TPU v7x, 32 devices: a whole 2x2x4 slice. The times are simulated.
32 devices in a mesh: loop: 4 (over x, core), blk: 8 (over z, y).
Axes of the slice: x: 2, y: 2, z: 4, core: 2. Of those that a mesh axis runs over, the one named last changes fastest.
Arguments:
- user_factors: float32 [4, 8, 1024, 512], P('loop', 'blk'), may hold values from -0.4 to 0.4
- blocks: float32 [4, 8, 2, 512, 512], P('loop', 'blk'), may hold values from -0.4 to 0.4
- user_tile: int32 [4, 8, 4, 12], P('loop', 'blk'), may hold values from 0 to 7
- item_tile: int32 [4, 8, 4, 12], P('loop', 'blk'), may hold values from 0 to 7
- ratings: bfloat16 [4, 8, 4, 12, 128, 128], P('loop', 'blk'), may hold values from -6 to 6
- dest_loop: int32 [4, 8, 2], P(None, 'blk'), may hold values from 0 to 3, as said below
Outputs:
- user_result: float32 [4, 8, 1024, 512], P('loop', 'blk')
- block_result: float32 [4, 8, 2, 512, 512], P('loop', 'blk')
Inputs may be any that keep to these rules, and one draw needn't show every extreme that they name: `dest_loop`: for each shard index c: every loop receives exactly 2 blocks of index c; two loops send both their blocks to one loop each, and the other two loops each send one block to each of the two remaining loops.
All inputs are finite; a program needn't handle non-finite values.
Results may differ from a plain program's by a relative error of at most 0.0003.
Values sent between devices are 32-bit elements; how exact they have to be, the bound alone decides.
A program may use at most 128 MiB of HBM per device.

v0:
```python
import functools

import jax
import jax.numpy as jnp
from jax import lax
from jax.experimental import pallas as pl
from jax.experimental.pallas import tpu as pltpu
from jax.sharding import PartitionSpec as P

learn_rate = 0.01
keep_rate = 0.98
MESH = pl.DeviceIdType.MESH
GROUP = 2


def split(x):
    high = x.astype(jnp.bfloat16)
    return high, (x - high.astype(jnp.float32)).astype(jnp.bfloat16)


def dot3(a, b, dims):
    dot = functools.partial(
        lax.dot_general,
        dimension_numbers=(dims, ((), ())),
        preferred_element_type=jnp.float32,
    )
    return dot(a[0], b[0]) + (dot(a[0], b[1]) + dot(a[1], b[0]))


def picks(hits, ranks, places, count):
    chosen = [jnp.int32(0)] * count
    for hit, rank, place in zip(hits, ranks, places):
        for wanted in range(count):
            chosen[wanted] = jnp.where(hit & (rank == wanted), place, chosen[wanted])
    return chosen


def kernel(visits, chunks, slots, tile, loops, columns, *refs):
    refs = list(refs)
    take = lambda n: [refs.pop(0) for _ in range(n)]
    ut, it, routes, u_ref, h_ref, r_ref, uo, ho = take(8)
    arrived = take(visits - 1)
    updated = take(visits - 1)
    cand, stage, got, fin = take(chunks), take(chunks), take(chunks), take(chunks)
    uh, ul, qh, ql, fsum = take(5)
    y_send, y_recv, x_send, x_recv, c_send, c_recv = take(6)

    held = h_ref.shape[0]
    rank_width = u_ref.shape[-1]
    width = held * tile
    step = GROUP * tile
    row_steps = u_ref.shape[0] // step
    midway = visits // 2 - 1

    me, col = lax.axis_index("loop"), lax.axis_index("blk")
    far = (me + 2) % loops
    near = me + 1 - 2 * (me % 2)
    diagonal = (near + 2) % loops
    right, left = (col + 1) % columns, (col + columns - 1) % columns

    barrier = pltpu.get_barrier_semaphore()
    for target in ((me, left), (far, col), (near, col)):
        pl.semaphore_signal(barrier, inc=1, device_id=target, device_id_type=MESH)

    mine = [(me, s) for s in range(held)] + [(far, s) for s in range(held)]
    theirs = [(near, s) for s in range(held)] + [(diagonal, s) for s in range(held)]

    def ranks_of(hits):
        seen, ranks = jnp.int32(0), []
        for hit in hits:
            ranks.append(seen)
            seen = seen + hit.astype(jnp.int32)
        return ranks

    to_near = [routes[a, s] == near for a, s in mine]
    near_pick = picks(to_near, ranks_of(to_near), range(2 * held), held)
    items = mine + theirs
    to_me = [routes[a, s] == me for a, s in items]
    labels = [a * held + s for a, s in items]
    their_ranks = ranks_of(to_me[2 * held :])
    places = list(range(2 * held)) + [2 * held + r for r in their_ranks]
    all_ranks = []
    for label in labels:
        before = jnp.int32(0)
        for other, hit in zip(labels, to_me):
            before = before + (hit & (other < label)).astype(jnp.int32)
        all_ranks.append(before)
    final_pick = picks(to_me, all_ranks, places, held)

    pl.semaphore_wait(barrier, 3)

    def rows_of(c):
        return pl.ds(pl.multiple_of(c * tile, tile), tile)

    def y_copy(v, c, src=None):
        return pltpu.make_async_remote_copy(
            src_ref=updated[v].at[:, rows_of(c), :] if src is None else src,
            dst_ref=arrived[v].at[:, rows_of(c), :],
            send_sem=y_send.at[v, c],
            recv_sem=y_recv.at[v, c],
            device_id=(me, right),
            device_id_type=MESH,
        )

    def x_copy(c):
        return pltpu.make_async_remote_copy(
            src_ref=cand[c].at[pl.ds(0, held)],
            dst_ref=cand[c].at[pl.ds(held, held)],
            send_sem=x_send.at[c],
            recv_sem=x_recv.at[c],
            device_id=(far, col),
            device_id_type=MESH,
        )

    def c_copy(c):
        return pltpu.make_async_remote_copy(
            src_ref=stage[c],
            dst_ref=got[c],
            send_sem=c_send.at[c],
            recv_sem=c_recv.at[c],
            device_id=(near, col),
            device_id_type=MESH,
        )

    def begin_users(v):
        def body(m, _):
            rows = pl.ds(pl.multiple_of(m * step, step), step)
            users = u_ref[rows, :] if v == 0 else uo[rows, :]
            uh[rows, :], ul[rows, :] = split(users)
            uo[rows, :] = keep_rate * users
            return 0

        lax.fori_loop(0, row_steps, body, 0)

    def update_chunk(v, c, q, write):
        q = q.reshape(width, rank_width)
        qh[...], ql[...] = split(q)
        fsum[...] = keep_rate * q

        def body(m, _):
            rows = pl.ds(pl.multiple_of(m * step, step), step)
            users = (uh[rows, :], ul[rows, :])
            blocks = (qh[...], ql[...])
            guessed = dot3(users, blocks, ((1,), (1,)))
            lines = []
            for a in range(GROUP):
                line = []
                for b in range(held):
                    total = jnp.zeros((tile, tile), jnp.float32)
                    count = jnp.float32(0)
                    for k in range(slots):
                        named = (ut[v, k] == m * GROUP + a) & (it[v, k] == b * chunks + c)
                        weight = jnp.where(named, jnp.float32(1), jnp.float32(0))
                        total = total + weight * r_ref[v, k].astype(jnp.float32)
                        count = count + weight
                    part = guessed[a * tile : (a + 1) * tile, b * tile : (b + 1) * tile]
                    line.append(total - count * part)
                lines.append(jnp.concatenate(line, axis=1))
            errors = split(jnp.concatenate(lines, axis=0))
            uo[rows, :] = uo[rows, :] + learn_rate * dot3(errors, blocks, ((1,), (0,)))
            fsum[...] = fsum[...] + learn_rate * dot3(errors, users, ((0,), (0,)))
            return 0

        lax.fori_loop(0, row_steps, body, 0)
        write(fsum[...].reshape(held, tile, rank_width))

    def relocate(c):
        x_copy(c).wait_recv()
        for r in range(held):
            stage[c][r] = cand[c][near_pick[r]]
        c_copy(c).start()
        c_copy(c).wait_recv()
        for r in range(held):
            place = final_pick[r]
            own = cand[c][jnp.minimum(place, 2 * held - 1)]
            other = got[c][jnp.maximum(place - 2 * held, 0)]
            fin[c][r] = jnp.where(place < 2 * held, own, other)
        y_copy(midway, c, fin[c]).start()

    for v in range(visits):
        begin_users(v)

        def read(c):
            if v == 0:
                return h_ref[:, rows_of(c), :]
            landed = arrived[v - 1].at[:, rows_of(c), :]
            y_copy(v - 1, c, landed).wait_recv()
            return arrived[v - 1][:, rows_of(c), :]

        if v == midway:
            for c in range(chunks):

                def write(value, c=c):
                    cand[c][pl.ds(0, held)] = value

                update_chunk(v, c, read(c), write)
                x_copy(c).start()
                if c >= 1:
                    relocate(c - 1)
            relocate(chunks - 1)
        else:
            target = ho if v == visits - 1 else updated[v]

            def chunk_body(c, _):
                def write(value):
                    target[:, rows_of(c), :] = value

                update_chunk(v, c, read(c), write)
                if v < visits - 1:
                    y_copy(v, c).start()
                return 0

            lax.fori_loop(0, chunks, chunk_body, 0)

    for c in range(chunks):
        for v in range(visits - 1):
            y_copy(v, c, fin[c] if v == midway else None).wait_send()
        x_copy(c).wait_send()
        c_copy(c).wait_send()


def on_device(loops, columns, user_factors, blocks, user_tile, item_tile, ratings, dest_loop):
    users, held_blocks = user_factors[0, 0], blocks[0, 0]
    user_index, item_index, tiles = user_tile[0, 0], item_tile[0, 0], ratings[0, 0]
    routes = dest_loop[:, 0, :]
    visits, slots, tile, _ = tiles.shape
    held, block_rows, rank_width = held_blocks.shape
    chunks = block_rows // tile
    assert loops == 4 and visits >= 2 and users.shape[0] % (GROUP * tile) == 0
    pieces = lambda n: [pltpu.VMEM((n * held, tile, rank_width), jnp.float32)] * chunks
    whole = pltpu.VMEM(held_blocks.shape, jnp.float32)
    vmem = pl.BlockSpec(memory_space=pltpu.VMEM)
    smem = pl.BlockSpec(memory_space=pltpu.SMEM)
    new_users, new_blocks = pl.pallas_call(
        functools.partial(kernel, visits, chunks, slots, tile, loops, columns),
        out_shape=(
            jax.ShapeDtypeStruct(users.shape, jnp.float32),
            jax.ShapeDtypeStruct(held_blocks.shape, jnp.float32),
        ),
        in_specs=[smem, smem, smem, vmem, vmem, vmem],
        out_specs=(vmem, vmem),
        scratch_shapes=[whole] * (2 * (visits - 1))
        + pieces(2)
        + pieces(1) * 3
        + [pltpu.VMEM(users.shape, jnp.bfloat16)] * 2
        + [pltpu.VMEM((held * tile, rank_width), jnp.bfloat16)] * 2
        + [pltpu.VMEM((held * tile, rank_width), jnp.float32)]
        + [pltpu.SemaphoreType.DMA((visits - 1, chunks))] * 2
        + [pltpu.SemaphoreType.DMA((chunks,))] * 4,
        compiler_params=pltpu.CompilerParams(
            collective_id=0, has_side_effects=True, vmem_limit_bytes=56 * 2**20
        ),
    )(user_index, item_index, routes, users, held_blocks, tiles)
    return new_users[None, None], new_blocks[None, None]


def solution(mesh):
    placed = (
        P("loop", "blk", None, None),
        P("loop", "blk", None, None, None),
        P("loop", "blk", None, None),
        P("loop", "blk", None, None),
        P("loop", "blk", None, None, None, None),
        P(None, "blk", None),
    )
    return jax.shard_map(
        functools.partial(on_device, mesh.shape["loop"], mesh.shape["blk"]),
        mesh=mesh,
        in_specs=placed,
        out_specs=(P("loop", "blk", None, None), P("loop", "blk", None, None, None)),
        check_vma=False,
    )
```

profile of v0, /device:TPU:0, one launch (start us, length us, event | category | flops | bytes accessed | tf_op | source)
XLA Modules:
  0.0 166.3 jit_solution(12346019174586231445)
XLA Ops:
  0.6 1.3 copy.8.refs_2_
  2.0 159.8 %shard_map.77 = (f32[1024,512]{1,0:T(8,128)}, f32[2,512,512]{2,1,0:T(8,128)}) custom-call(s32[4,12]{1,0:T(4,128)} %bitcast.13, s32[4,12]{1,0:T(4,128)} %bitcast.14, s32[4,2]{1,0:T(4,128)} %copy.8.refs_2_, f32[1024,512]{1,0:T(8,128)} %bitcast.8, f32[2,512,512]{2,1,0:T(8,128)} %bitcast.9, bf16[4,12,128,128]{3,2,1,0:T(8,128)(2,1)} %bitcast.12), custom_call_target="tpu_custom_call" | custom-call | tf_op jit(solution)/shard_map/pallas_call | solution.py:234
  161.7 0.0 copy-start
  161.7 3.2 %copy.11 = f32[1,1,1024,512]{3,2,1,0:T(8,128)} copy(f32[1,1,1024,512]{3,2,1,0:T(8,128)} %bitcast.11) | data formatting | bytes 4194304
  165.0 0.0 copy-done
  165.0 1.3 copy.12
Async XLA Ops:
  161.7 3.2 %copy-start = (f32[2,512,512]{2,1,0:T(8,128)S(1)}, f32[2,512,512]{2,1,0:T(8,128)}, u32[]{:S(2)}) copy-start(f32[2,512,512]{2,1,0:T(8,128)} %get-tuple-element.5) | copy-start | bytes 6291460
where the time goes:
time: 166 us
  Pallas kernels  160 us (96%)
  local copies, waits for them, and re-layouts  5.89 us (4%)
    pallas_call x1, Pallas kernels, on_device(): pl.pallas_call(functools.partial(kernel, visits, chunks, slots, tile, loo...  160 us
    unnamed x4, local copies, waits for them, and re-layouts  4.55 us

commit v1 on v0

--- a/solution.py
+++ b/solution.py
@@ -1,4 +1,5 @@
 import functools
+import math
 
 import jax
 import jax.numpy as jnp
@@ -10,7 +11,7 @@
 learn_rate = 0.01
 keep_rate = 0.98
 MESH = pl.DeviceIdType.MESH
-GROUP = 2
+GROUP = 8
 
 
 def split(x):
@@ -42,14 +43,16 @@
     arrived = take(visits - 1)
     updated = take(visits - 1)
     cand, stage, got, fin = take(chunks), take(chunks), take(chunks), take(chunks)
-    uh, ul, qh, ql, fsum = take(5)
+    uh, ul, qh, ql, sums, counts = take(6)
     y_send, y_recv, x_send, x_recv, c_send, c_recv = take(6)
 
     held = h_ref.shape[0]
     rank_width = u_ref.shape[-1]
     width = held * tile
-    step = GROUP * tile
-    row_steps = u_ref.shape[0] // step
+    user_tiles = u_ref.shape[0] // tile
+    group = math.gcd(GROUP, user_tiles)
+    step = group * tile
+    row_steps = user_tiles // group
     midway = visits // 2 - 1
 
     me, col = lax.axis_index("loop"), lax.axis_index("blk")
@@ -72,10 +75,10 @@
             seen = seen + hit.astype(jnp.int32)
         return ranks
 
-    to_near = [routes[a, s] == near for a, s in mine]
+    to_near = [routes[s, a] == near for a, s in mine]
     near_pick = picks(to_near, ranks_of(to_near), range(2 * held), held)
     items = mine + theirs
-    to_me = [routes[a, s] == me for a, s in items]
+    to_me = [routes[s, a] == me for a, s in items]
     labels = [a * held + s for a, s in items]
     their_ranks = ranks_of(to_me[2 * held :])
     places = list(range(2 * held)) + [2 * held + r for r in their_ranks]
@@ -87,8 +90,6 @@
         all_ranks.append(before)
     final_pick = picks(to_me, all_ranks, places, held)
 
-    pl.semaphore_wait(barrier, 3)
-
     def rows_of(c):
         return pl.ds(pl.multiple_of(c * tile, tile), tile)
 
@@ -122,47 +123,61 @@
             device_id_type=MESH,
         )
 
+    kept = lambda v: keep_rate / learn_rate if v == visits - 1 else keep_rate
+    rated = lambda v, x: x if v == visits - 1 else learn_rate * x
+
     def begin_users(v):
         def body(m, _):
             rows = pl.ds(pl.multiple_of(m * step, step), step)
             users = u_ref[rows, :] if v == 0 else uo[rows, :]
             uh[rows, :], ul[rows, :] = split(users)
-            uo[rows, :] = keep_rate * users
+            uo[rows, :] = kept(v) * users
             return 0
 
         lax.fori_loop(0, row_steps, body, 0)
+
+    def build(v, c):
+        def body(t, _):
+            rows = pl.ds(pl.multiple_of(t * tile, tile), tile)
+            for b in range(held):
+                total = jnp.zeros((tile, tile), jnp.float32)
+                count = jnp.float32(0)
+                for k in range(slots):
+                    named = (ut[v, k] == t) & (it[v, k] == b * chunks + c)
+                    weight = jnp.where(named, jnp.float32(1), jnp.float32(0))
+                    total = total + weight * r_ref[v, k].astype(jnp.float32)
+                    count = count + weight
+                sums[rows, pl.ds(b * tile, tile)] = total
+                counts[t, b] = count
+            return 0
+
+        lax.fori_loop(0, user_tiles, body, 0)
 
     def update_chunk(v, c, q, write):
         q = q.reshape(width, rank_width)
         qh[...], ql[...] = split(q)
-        fsum[...] = keep_rate * q
-
-        def body(m, _):
+
+        def body(m, fsum):
             rows = pl.ds(pl.multiple_of(m * step, step), step)
             users = (uh[rows, :], ul[rows, :])
             blocks = (qh[...], ql[...])
             guessed = dot3(users, blocks, ((1,), (1,)))
             lines = []
-            for a in range(GROUP):
+            for a in range(group):
                 line = []
                 for b in range(held):
-                    total = jnp.zeros((tile, tile), jnp.float32)
-                    count = jnp.float32(0)
-                    for k in range(slots):
-                        named = (ut[v, k] == m * GROUP + a) & (it[v, k] == b * chunks + c)
-                        weight = jnp.where(named, jnp.float32(1), jnp.float32(0))
-                        total = total + weight * r_ref[v, k].astype(jnp.float32)
-                        count = count + weight
                     part = guessed[a * tile : (a + 1) * tile, b * tile : (b + 1) * tile]
-                    line.append(total - count * part)
+                    line.append(counts[m * group + a, b] * part)
                 lines.append(jnp.concatenate(line, axis=1))
-            errors = split(jnp.concatenate(lines, axis=0))
-            uo[rows, :] = uo[rows, :] + learn_rate * dot3(errors, blocks, ((1,), (0,)))
-            fsum[...] = fsum[...] + learn_rate * dot3(errors, users, ((0,), (0,)))
-            return 0
-
-        lax.fori_loop(0, row_steps, body, 0)
-        write(fsum[...].reshape(held, tile, rank_width))
+            errors = split(sums[rows, :] - jnp.concatenate(lines, axis=0))
+            uo[rows, :] = uo[rows, :] + rated(v, dot3(errors, blocks, ((1,), (0,))))
+            return fsum + rated(v, dot3(errors, users, ((0,), (0,))))
+
+        if row_steps == 1:
+            fsum = body(0, kept(v) * q)
+        else:
+            fsum = lax.fori_loop(0, row_steps, body, kept(v) * q)
+        write(fsum.reshape(held, tile, rank_width))
 
     def relocate(c):
         x_copy(c).wait_recv()
@@ -177,6 +192,7 @@
             fin[c][r] = jnp.where(place < 2 * held, own, other)
         y_copy(midway, c, fin[c]).start()
 
+    build(0, 0)
     for v in range(visits):
         begin_users(v)
 
@@ -194,9 +210,14 @@
                     cand[c][pl.ds(0, held)] = value
 
                 update_chunk(v, c, read(c), write)
+                if v == 0 and c == 0:
+                    pl.semaphore_wait(barrier, 3)
                 x_copy(c).start()
+                if c + 1 < chunks:
+                    build(v, c + 1)
                 if c >= 1:
                     relocate(c - 1)
+            build(v + 1, 0)
             relocate(chunks - 1)
         else:
             target = ho if v == visits - 1 else updated[v]
@@ -207,10 +228,23 @@
 
                 update_chunk(v, c, read(c), write)
                 if v < visits - 1:
+                    if v == 0:
+
+                        @pl.when(c == 0)
+                        def _():
+                            pl.semaphore_wait(barrier, 3)
+
                     y_copy(v, c).start()
                 return 0
 
-            lax.fori_loop(0, chunks, chunk_body, 0)
+            def step_body(c, _):
+                build(v, c)
+                return chunk_body(c, 0)
+
+            chunk_body(jnp.int32(0), 0)
+            lax.fori_loop(1, chunks, step_body, 0)
+            if v < visits - 1:
+                build(v + 1, 0)
 
     for c in range(chunks):
         for v in range(visits - 1):
@@ -222,11 +256,11 @@
 def on_device(loops, columns, user_factors, blocks, user_tile, item_tile, ratings, dest_loop):
     users, held_blocks = user_factors[0, 0], blocks[0, 0]
     user_index, item_index, tiles = user_tile[0, 0], item_tile[0, 0], ratings[0, 0]
-    routes = dest_loop[:, 0, :]
+    routes = dest_loop[:, 0, :].T
     visits, slots, tile, _ = tiles.shape
     held, block_rows, rank_width = held_blocks.shape
     chunks = block_rows // tile
-    assert loops == 4 and visits >= 2 and users.shape[0] % (GROUP * tile) == 0
+    assert loops == 4 and visits >= 2 and users.shape[0] % tile == 0
     pieces = lambda n: [pltpu.VMEM((n * held, tile, rank_width), jnp.float32)] * chunks
     whole = pltpu.VMEM(held_blocks.shape, jnp.float32)
     vmem = pl.BlockSpec(memory_space=pltpu.VMEM)
@@ -244,14 +278,15 @@
         + pieces(1) * 3
         + [pltpu.VMEM(users.shape, jnp.bfloat16)] * 2
         + [pltpu.VMEM((held * tile, rank_width), jnp.bfloat16)] * 2
-        + [pltpu.VMEM((held * tile, rank_width), jnp.float32)]
+        + [pltpu.VMEM((users.shape[0], held * tile), jnp.float32)]
+        + [pltpu.SMEM((users.shape[0] // tile, held), jnp.float32)]
         + [pltpu.SemaphoreType.DMA((visits - 1, chunks))] * 2
         + [pltpu.SemaphoreType.DMA((chunks,))] * 4,
         compiler_params=pltpu.CompilerParams(
             collective_id=0, has_side_effects=True, vmem_limit_bytes=56 * 2**20
         ),
     )(user_index, item_index, routes, users, held_blocks, tiles)
-    return new_users[None, None], new_blocks[None, None]
+    return learn_rate * new_users[None, None], learn_rate * new_blocks[None, None]
 
 
 def solution(mesh):

time: 166 us -> 162 us (0.976)
  local copies, waits for them, and re-layouts: 5.89 us -> 0.01 us
  other arithmetic: 0 us -> 4.88 us
  Pallas kernels: 160 us -> 156 us
    mul x0 -> x2, other arithmetic: none -> 4.88 us  [the longest x1 3.3 us: on_device(): learn_rate * new_users[None, None]]
    unnamed x4 -> x2, local copies, waits for them, and re-layouts: 4.55 us -> 0.01 us
    pallas_call x1, Pallas kernels: 160 us -> 156 us  [on_device(): pl.pallas_call(functools.partial(kernel, visits, chunks, slots, tile, loo...]
where the time goes in v1:
time: 162 us
  Pallas kernels  156 us (96%)
  other arithmetic  4.88 us (3%)
    pallas_call x1, Pallas kernels, on_device(): pl.pallas_call(functools.partial(kernel, visits, chunks, slots, tile, loo...  156 us
    mul x1, other arithmetic, on_device(): learn_rate * new_users[None, None]  3.3 us

profile of v1, /device:TPU:0, one launch (start us, length us, event | category | flops | bytes accessed | tf_op | source)
XLA Modules:
  0.0 161.8 jit_solution(7206650508735328752)
XLA Ops:
  0.6 156.2 %shard_map.77 = (f32[1024,512]{1,0:T(8,128)}, f32[2,512,512]{2,1,0:T(8,128)}) custom-call(s32[4,12]{1,0:T(4,128)} %bitcast.15, s32[4,12]{1,0:T(4,128)} %bitcast.16, s32[2,4]{1,0:T(2,128)} %bitcast.17, f32[1024,512]{1,0:T(8,128)} %bitcast.12, f32[2,512,512]{2,1,0:T(8,128)} %bitcast.13, bf16[4,12,128,128]{3,2,1,0:T(8,128)(2,1)} %bitcast.14), custom_call_target="tpu_custom_call" | custom-call | tf_op jit(solution)/shard_map/pallas_call | solution.py:268
  156.9 0.0 copy-start
  156.9 3.3 %multiply_bitcast_fusion.1 = f32[1,1,1024,512]{3,2,1,0:T(8,128)} fusion(f32[1024,512]{1,0:T(8,128)} %get-tuple-element.4), kind=kLoop, calls=%fused_computation.1 | loop fusion | flops 524288 | bytes 4194304 | tf_op jit(solution)/shard_map/mul | solution.py:289
  160.2 0.0 copy-done
  160.2 1.6 multiply_bitcast_fusion
Async XLA Ops:
  156.9 3.3 %copy-start = (f32[2,512,512]{2,1,0:T(8,128)S(1)}, f32[2,512,512]{2,1,0:T(8,128)}, u32[]{:S(2)}) copy-start(f32[2,512,512]{2,1,0:T(8,128)} %get-tuple-element.5) | copy-start | bytes 6291460
